TPU v7x, 256 devices: a whole 4x4x8 slice. The times are simulated.
256 devices in a mesh: member: 8 (over x_lo, y), grid: 32 (over x_hi, z, core).
Axes of the slice: x: 4 (x_hi: 2, x_lo: 2; x = x_hi * 2 + x_lo), y: 4, z: 8, core: 2. Of those that a mesh axis runs over, the one named last changes fastest.
Arguments:
- latent: bfloat16 [8, 8192, 1024], P('member', 'grid'), may hold values from -6 to 6
- grid_latent_skip: bfloat16 [8, 16384, 1024], P('member', 'grid'), may hold values from -6 to 6
- initial_member_state: float32 [8, 100, 16384], P('member', None, 'grid'), may hold values from -6 to 6
- target: float32 [100, 16384], P(None, 'grid'), may hold values from -6 to 6
- neighbours: int32 [3, 16384], P(None, 'grid'), may hold values from 0 to 511, as said below
- edge_weight: float32 [3, 16384], P(None, 'grid'), may hold values from 0.2 to 1
- area_weight: float32 [16384], P('grid'), may hold values from 0.3 to 27, as said below
- variable_weight: float32 [100], replicated, may hold values from 0.3 to 3
- output_projection: bfloat16 [100, 1024], replicated, may hold values from -0.1875 to 0.1875
- layer_norm_gain: float32 [1024], replicated, may hold values from 0.1 to 1.9
Outputs:
- fair_crps: float32 [], replicated
- latent_grad: bfloat16 [8, 8192, 1024], P('member', 'grid')
- out_weight_grad: float32 [100, 1024], replicated
- norm_gain_grad: float32 [1024], replicated
Inputs may be any that keep to these rules, and one draw needn't show every extreme that they name: neighbours[k, p] indexes 256 + 2 * 128 rows ordered by latitude: the 128 last mesh rows of the slab below the point's slab, the slab's own 256 rows, then the 128 first rows of the slab above. `area_weight`: positive.
All inputs are finite; a program needn't handle non-finite values.
Results may differ from a plain program's by a relative error of at most 0.0067.
Values may be sent and summed in bfloat16 or wider, within the bound.
No kernel may reach another device: no remote copies, remote signals or barrier semaphores. Data moves between devices by JAX's collectives and lax.ppermute only.
A program may use at most 64 MiB of HBM per device.

v0:
```python
import jax
import jax.numpy as jnp
from jax import lax
from jax.sharding import PartitionSpec as P

SMOOTHING = 0.25
FAIRNESS = 0.95
norm_eps = 1e-05


def with_halo(array, sides, width):
    for axis, dim in sides:
        size, length = (lax.axis_size(axis), array.shape[dim])
        up = [(i, (i + 1) % size) for i in range(size - 1)]
        down = [(j, i) for i, j in up]
        last = lax.slice_in_dim(array, length - width, length, axis=dim)
        initial = lax.slice_in_dim(array, 0, width, axis=dim)
        before = lax.ppermute(last, axis, up)
        after = lax.ppermute(initial, axis, down)
        array = jnp.concatenate([before, array, after], axis=dim)
    return array


def from_behind(block, axis, distance):
    devices = range(lax.axis_size(axis))
    route = [(i - distance, i) for i in devices if i - distance in devices]
    return lax.ppermute(block, axis, route)


def smooth_abs(value):
    return jnp.sqrt(value * value + SMOOTHING * SMOOTHING)


def per_device(
    latent,
    grid_latent_skip,
    initial_member_state,
    target,
    neighbours,
    edge_weight,
    area_weight,
    variable_weight,
    output_projection,
    layer_norm_gain,
):
    mesh_count = latent.shape[1]
    rim = mesh_count // 2
    points = grid_latent_skip.shape[1]
    slots = neighbours.shape[0]
    variables = output_projection.shape[0]
    member_list = lax.axis_size("member")
    extended = with_halo(latent, (("grid", 1),), rim)[0]
    weight_arrays = edge_weight / jnp.sum(edge_weight, axis=0, keepdims=True)
    mixed = grid_latent_skip[0].astype(jnp.float32)
    for slot in range(slots):
        mixed = mixed + weight_arrays[slot][:, None] * jnp.take(
            extended, neighbours[slot], axis=0
        ).astype(jnp.float32)
    centred = mixed - jnp.mean(mixed, axis=1, keepdims=True)
    rscale = lax.rsqrt(jnp.mean(centred * centred, axis=1, keepdims=True) + norm_eps)
    normed = centred * rscale
    scaled = (normed * layer_norm_gain[None, :]).astype(jnp.bfloat16)
    predicted_field = initial_member_state[0] + lax.dot_general(
        output_projection, scaled, (((1,), (1,)), ((), ())), preferred_element_type=jnp.float32
    )
    weight_map = variable_weight[:, None] * area_weight[None, :]
    pair_distance = predicted_field - target
    spread = smooth_abs(pair_distance)
    eps_fair = (1.0 - FAIRNESS) / member_list
    coef_pair = (1.0 - eps_fair) / (member_list * (member_list - 1))
    every_member_set = lax.all_gather(predicted_field[None], "member", axis=0, tiled=True)
    member_difference = predicted_field[None] - every_member_set
    dist = smooth_abs(member_difference)
    pair_total = jnp.sum(dist, axis=0) - SMOOTHING
    pair_slope = jnp.sum(member_difference / dist, axis=0)
    pair_loss = jnp.sum(weight_map * pair_total)
    local_loss = jnp.sum(weight_map * spread) / member_list - 0.5 * coef_pair * pair_loss
    fore_grad = (
        weight_map * (pair_distance / spread / member_list - coef_pair * pair_slope)
    ).astype(jnp.bfloat16)
    wout_part = jnp.dot(fore_grad, scaled, preferred_element_type=jnp.float32)
    scaled_grad = lax.dot_general(
        fore_grad, output_projection, (((0,), (0,)), ((), ())), preferred_element_type=jnp.float32
    )
    gain_part = jnp.sum(scaled_grad * normed, axis=0)
    norm_grad = scaled_grad * layer_norm_gain[None, :]
    mixed_grad = rscale * (
        norm_grad
        - jnp.mean(norm_grad, axis=1, keepdims=True)
        - normed * jnp.mean(norm_grad * normed, axis=1, keepdims=True)
    )
    collect = jnp.zeros((extended.shape[0], extended.shape[1]), jnp.float32)
    for slot in range(slots):
        collect = collect.at[neighbours[slot]].add(weight_arrays[slot][:, None] * mixed_grad)
    from_above = from_behind(collect[:rim].astype(jnp.bfloat16), "grid", -1).astype(jnp.float32)
    from_below = from_behind(collect[rim + mesh_count :].astype(jnp.bfloat16), "grid", 1).astype(
        jnp.float32
    )
    owned = collect[rim : rim + mesh_count] + jnp.concatenate([from_below, from_above], axis=0)
    sums = lax.psum((wout_part, gain_part, local_loss), ("member", "grid"))
    fair_crps = sums[2] / (points * lax.axis_size("grid") * variables)
    return (fair_crps, owned[None].astype(jnp.bfloat16), sums[0], sums[1])


def solution(mesh):
    placed = (
        P("member", "grid", None),
        P("member", "grid", None),
        P("member", None, "grid"),
        P(None, "grid"),
        P(None, "grid"),
        P(None, "grid"),
        P("grid"),
        P(),
        P(),
        P(),
    )
    return jax.shard_map(
        per_device,
        mesh=mesh,
        in_specs=placed,
        out_specs=(P(), P("member", "grid", None), P(), P()),
        check_vma=False,
    )
```

profile of v0, /device:TPU:2, one launch (start us, length us, event | category | flops | bytes accessed | tf_op | source)
XLA Modules:
  0.0 378.3 jit_solution(10001090698908370508)
XLA Ops:
  7.2 0.0 copy-start
  7.2 0.0 all-gather.4.cloned.1.call-start
  7.2 1.1 fusion.24
  8.3 1.8 collective-permute-start
  10.1 1.3 collective-permute-start.1
  11.4 0.8 fusion.26
  12.3 0.7 reduce_sum.90
  13.0 0.7 broadcast_divide_fusion
  13.8 0.0 collective-permute-done
  13.8 1.5 collective-permute-done.1
  15.2 1.1 maximum_bitcast_fusion
  16.3 2.1 gather_fusion.2
  18.4 2.8 gather_fusion.1
  21.2 2.8 gather_fusion
  24.0 2.8 fusion.21
  26.8 0.0 copy-start.6
  26.8 0.3 multiply_reduce_fusion.2
  27.2 0.3 copy-done.6
  27.5 0.3 multiply_convert_fusion
  27.8 0.0 copy-done
  27.9 0.3 copy-done.4
  28.1 1.1 fusion.11
  29.3 0.0 all-gather.4.cloned.1.call-update
  29.3 0.0 all-reduce.3.cloned.1.call-start
  29.4 0.0 copy-done.7
  29.4 49.7 %all-gather.4.cloned.1.call-done = f32[8,100,512]{2,1,0:T(8,128)} async-done(((f32[1,100,512]{2,1,0:T(8,128)}), f32[8,100,512]{2,1,0:T(8,128)}) %all-gather.4.cloned.1.call-update) | async-done | bytes 1638416 | tf_op jit(solution)/shard_map/all_gather | solution.py:71
  79.0 2.5 fusion.10
  81.5 0.0 copy-done.8
  81.5 0.0 copy-done.9
  81.6 0.8 fusion.19
  82.4 0.9 multiply_reduce_fusion
  83.3 1.9 subtract_multiply_fusion
  85.2 7.4 %scatter_custom_fusion = f32[512,1024]{1,0:T(8,128)} fusion(s32[512]{0:T(512)S(1)} %bitcast.51, f32[512,1024]{1,0:T(8,128)} %subtract_multiply_fusion, f32[]{:T(128)} %constant.19.clone.1, f32[512]{0:T(512)S(1)} %bitcast.42), kind=kCustom, calls=%fused_computation.14 | custom fusion | flops 1048576 | bytes 4196356 | tf_op jit(solution)/shard_map/scatter-add | solution.py:94
  92.7 0.0 copy-done.1
  92.7 7.7 %scatter_custom_fusion.1 = f32[512,1024]{1,0:T(8,128)} fusion(f32[512,1024]{1,0:T(8,128)} %scatter_custom_fusion, s32[512]{0:T(512)S(1)} %bitcast.50, f32[512,1024]{1,0:T(8,128)S(1)} %copy-done.1, f32[512]{0:T(512)S(1)} %bitcast.40), kind=kCustom, calls=%fused_computation.12 | custom fusion | flops 1048576 | bytes 4196352 | tf_op jit(solution)/shard_map/scatter-add | solution.py:94
  100.4 7.7 %scatter_custom_fusion.2 = f32[512,1024]{1,0:T(8,128)} fusion(f32[512,1024]{1,0:T(8,128)} %scatter_custom_fusion.1, s32[512]{0:T(512)S(1)} %bitcast.49, f32[512,1024]{1,0:T(8,128)S(1)} %copy-done.1, f32[512]{0:T(512)S(1)} %bitcast.38), kind=kCustom, calls=%fused_computation.10 | custom fusion | flops 1048576 | bytes 4196352 | tf_op jit(solution)/shard_map/scatter-add | solution.py:94
  108.2 1.7 convert.6
  109.9 0.8 fusion.23
  110.8 2.0 collective-permute-start.2
  112.7 1.3 collective-permute-start.3
  114.0 1.1 fusion.27
  115.1 0.0 all-reduce.3.cloned.1.call-update
  116.4 79.3 %all-reduce = (f32[]{:T(128)}, f32[1024]{0:T(1024)}) all-reduce(f32[]{:T(128)S(6)} %sub.46, f32[1024]{0:T(1024)S(1)} %get-tuple-element.5), channel_id=1, replica_groups=mesh['member'=8,'grid'=32] {'member','grid'}, use_global_device_ids=true, to_apply=%region_6.8 | all-reduce | flops 1025 | bytes 8200 | tf_op jit(solution)/shard_map/psum | solution.py:100
  196.3 0.0 collective-permute-done.2
  196.3 0.0 collective-permute-done.3
  196.4 2.0 fusion.17
  198.3 170.2 %all-reduce.3.cloned.1.call-done = f32[100,1024]{1,0:T(8,128)} async-done(((f32[100,1024]{1,0:T(8,128)}), f32[100,1024]{1,0:T(8,128)}) %all-reduce.3.cloned.1.call-update) | async-done | bytes 409616 | tf_op jit(solution)/shard_map/psum | solution.py:100
  368.6 1.8 copy.19
  (25 shorter events, 0.1 us)
Async XLA Ops:
  7.2 20.7 %copy-start = (bf16[100,1024]{1,0:T(8,128)(2,1)S(1)}, bf16[100,1024]{1,0:T(8,128)(2,1)}, u32[]{:S(2)}) copy-start(bf16[100,1024]{1,0:T(8,128)(2,1)} %param.20) | copy-start | bytes 614404
  7.2 71.9 %all-gather.4.cloned.1.call-start = ((), (), s32[]{:S(2)}) async-start(), calls=%async_computation.1 | async-start | bytes 1916928 | tf_op jit(solution)/shard_map/all_gather | solution.py:71
  8.3 5.4 %collective-permute-start = (bf16[1,128,1024]{2,1,0:T(8,128)(2,1)S(1)}, bf16[1,128,1024]{2,1,0:T(8,128)(2,1)S(1)}, u32[]{:S(2)}, u32[]{:S(2)}) collective-permute-start(bf16[1,128,1024]{2,1,0:T(8,128)(2,1)S(1)} %get-tuple-element.18), channel_id=1, source_target_pairs={{0,1},{1,2},{2,3},{3,4},{4,5},{5,6},{6,7},{7,8},{8,9},{9,10},{10,1... | collective-permute-start | bytes 786440 | tf_op jit(solution)/shard_map/ppermute | solution.py:18
  10.1 5.1 %collective-permute-start.1 = (bf16[1,128,1024]{2,1,0:T(8,128)(2,1)S(1)}, bf16[1,128,1024]{2,1,0:T(8,128)(2,1)S(1)}, u32[]{:S(2)}, u32[]{:S(2)}) collective-permute-start(bf16[1,128,1024]{2,1,0:T(8,128)(2,1)S(1)} %get-tuple-element.19), channel_id=1, source_target_pairs={{1,0},{2,1},{3,2},{4,3},{5,4},{6,5},{7,6},{8,7},{9,8},{10,9},{11,1... | collective-permute-start | bytes 786440 | tf_op jit(solution)/shard_map/ppermute | solution.py:19
  26.8 0.7 copy-start.6
  27.2 0.9 copy-start.4
  27.5 1.8 copy-start.7
  28.1 53.4 %copy-start.8 = (f32[512]{0:T(512)S(1)}, f32[512]{0:T(512)}, u32[]{:S(2)}) copy-start(f32[512]{0:T(512)} %param.18) | copy-start | bytes 6148
  28.1 53.4 %copy-start.9 = (f32[100]{0:T(128)S(1)}, f32[100]{0:T(128)}, u32[]{:S(2)}) copy-start(f32[100]{0:T(128)} %param.19) | copy-start | bytes 1204
  29.3 339.3 %all-reduce.3.cloned.1.call-start = ((), (), s32[]{:S(2)}) async-start(), calls=%async_computation | async-start | bytes 851968 | tf_op jit(solution)/shard_map/psum | solution.py:100
  79.0 2.5 copy-start.3
  79.0 2.5 copy-start.5
  85.2 7.5 %copy-start.1 = (f32[512,1024]{1,0:T(8,128)S(1)}, f32[512,1024]{1,0:T(8,128)}, u32[]{:S(2)}) copy-start(f32[512,1024]{1,0:T(8,128)} %subtract_multiply_fusion) | copy-start | bytes 6291460
  109.9 86.4 %copy-start.2 = (f32[512,1024]{1,0:T(8,128)S(1)}, f32[512,1024]{1,0:T(8,128)}, u32[]{:S(2)}) copy-start(f32[512,1024]{1,0:T(8,128)} %scatter_custom_fusion.2) | copy-start | bytes 6291460
  110.8 85.6 %collective-permute-start.2 = (bf16[128,1024]{1,0:T(8,128)(2,1)}, bf16[128,1024]{1,0:T(8,128)(2,1)}, u32[]{:S(2)}, u32[]{:S(2)}) collective-permute-start(bf16[128,1024]{1,0:T(8,128)(2,1)} %get-tuple-element.16), channel_id=1, source_target_pairs={{0,1},{1,2},{2,3},{3,4},{4,5},{5,6},{6,7},{7,8},{8,9},{9,10},{10,1... | collective-permute-start | bytes 786440 | tf_op jit(solution)/shard_map/ppermute | solution.py:27
  112.7 83.6 %collective-permute-start.3 = (bf16[128,1024]{1,0:T(8,128)(2,1)}, bf16[128,1024]{1,0:T(8,128)(2,1)}, u32[]{:S(2)}, u32[]{:S(2)}) collective-permute-start(bf16[128,1024]{1,0:T(8,128)(2,1)} %get-tuple-element.17), channel_id=1, source_target_pairs={{1,0},{2,1},{3,2},{4,3},{5,4},{6,5},{7,6},{8,7},{9,8},{10,9},{11,1... | collective-permute-start | bytes 786440 | tf_op jit(solution)/shard_map/ppermute | solution.py:27
Sparse Core Ops, SparseCore 0:
  29.4 49.5 all-gather.3
  115.2 253.2 all-reduce.2
where the time goes:
time: 379 us; the launch traced here: 378 us
  waiting for transfers between devices  221 us (58%)
  blocking collectives  79.3 us (21%)
  other arithmetic  38 us (10%)
  between operations  17.4 us (5%)
  local copies, waits for them, and re-layouts  12.8 us (3%)
  starting transfers between devices  6.4 us (2%)
    psum x1, waiting for transfers between devices, per_device(): sums = lax.psum((wout_part, gain_part, local_loss), ('member', 'grid'))  170 us
    psum x1, blocking collectives, per_device(): sums = lax.psum((wout_part, gain_part, local_loss), ('member', 'grid'))  79.3 us
    all_gather x1, waiting for transfers between devices, per_device(): lax.all_gather(predicted_field[None], 'member', axis=0, tiled=True)  49.7 us
    scatter-add x3, other arithmetic, per_device(): collect.at[neighbours[slot]].add(weight_arrays[slot][:, None] * mixed_grad)  22.9 us
    gather x3, local copies, waits for them, and re-layouts, per_device(): jnp.take(extended, neighbours[slot], axis=0).astype(jnp.float32)  7.64 us
  transfers between devices with their start and end apart: 6, of which 3 were waited for; matrix products, arithmetic and copies ran while one was open for 1% of the time, Pallas kernels for 0%

commit v1 on v0

--- a/solution.py
+++ b/solution.py
@@ -97,7 +97,7 @@
         jnp.float32
     )
     owned = collect[rim : rim + mesh_count] + jnp.concatenate([from_below, from_above], axis=0)
-    sums = lax.psum((wout_part, gain_part, local_loss), ("member", "grid"))
+    sums = lax.psum(lax.psum((wout_part, gain_part, local_loss), "member"), "grid")
     fair_crps = sums[2] / (points * lax.axis_size("grid") * variables)
     return (fair_crps, owned[None].astype(jnp.bfloat16), sums[0], sums[1])
 

time: 379 us -> 437 us (1.15)
  waiting for transfers between devices: 221 us -> 272 us
  blocking collectives: 79.3 us -> 86.3 us
    psum x1 -> x2, waiting for transfers between devices: 170 us -> 221 us  [the longest x1 174 us: per_device(): lax.psum(lax.psum((wout_part, gain_part, local_loss), 'member'), 'grid')]
    psum x1 -> x2, blocking collectives: 79.3 us -> 86.3 us  [the longest x1 66.7 us: per_device(): lax.psum(lax.psum((wout_part, gain_part, local_loss), 'member'), 'grid')]
  transfers between devices with their start and end apart: 6 -> 7, of which waited for: 3 -> 4; matrix products, arithmetic and copies ran while one was open for 1% -> 7% of each run, Pallas kernels for 0% -> 0%
where the time goes in v1:
time: 437 us; the launch traced here: 436 us
  waiting for transfers between devices  272 us (62%)
  blocking collectives  86.3 us (20%)
  other arithmetic  38.7 us (9%)
  between operations  17.1 us (4%)
  local copies, waits for them, and re-layouts  12 us (3%)
  starting transfers between devices  5.95 us (1%)
    psum x1, waiting for transfers between devices, per_device(): lax.psum(lax.psum((wout_part, gain_part, local_loss), 'member'), 'grid')  174 us
    psum x1, blocking collectives, per_device(): lax.psum(lax.psum((wout_part, gain_part, local_loss), 'member'), 'grid')  66.7 us
    all_gather x1, waiting for transfers between devices, per_device(): lax.all_gather(predicted_field[None], 'member', axis=0, tiled=True)  49.6 us
    psum x1, waiting for transfers between devices, per_device(): lax.psum((wout_part, gain_part, local_loss), 'member')  46.8 us
    scatter-add x3, other arithmetic, per_device(): collect.at[neighbours[slot]].add(weight_arrays[slot][:, None] * mixed_grad)  23 us
    psum x1, blocking collectives, per_device(): lax.psum((wout_part, gain_part, local_loss), 'member')  19.6 us
  transfers between devices with their start and end apart: 7, of which 4 were waited for; matrix products, arithmetic and copies ran while one was open for 7% of the time, Pallas kernels for 0%

profile of v1, /device:TPU:2, one launch (start us, length us, event | category | flops | bytes accessed | tf_op | source)
XLA Modules:
  0.0 436.1 jit_solution(16454959256236815989)
XLA Ops:
  7.2 0.0 copy-start
  7.2 0.0 all-gather.4.cloned.1.call-start
  7.2 1.1 fusion.24
  8.3 1.8 collective-permute-start
  10.1 1.3 collective-permute-start.1
  11.4 0.8 fusion.26
  12.3 0.7 reduce_sum.90
  13.0 0.7 broadcast_divide_fusion
  13.8 0.0 collective-permute-done
  13.8 1.5 collective-permute-done.1
  15.2 1.1 maximum_bitcast_fusion
  16.3 2.1 gather_fusion.2
  18.4 2.8 gather_fusion.1
  21.2 2.8 gather_fusion
  24.0 2.8 fusion.21
  26.8 0.0 copy-start.6
  26.8 0.3 multiply_reduce_fusion.2
  27.2 0.3 copy-done.6
  27.5 0.3 multiply_convert_fusion
  27.8 0.0 copy-done
  27.9 0.3 copy-done.4
  28.1 1.1 fusion.11
  29.3 0.0 all-gather.4.cloned.1.call-update
  29.3 0.0 all-reduce.5.cloned.1.call-start
  29.4 0.0 copy-done.7
  29.4 49.6 %all-gather.4.cloned.1.call-done = f32[8,100,512]{2,1,0:T(8,128)} async-done(((f32[1,100,512]{2,1,0:T(8,128)}), f32[8,100,512]{2,1,0:T(8,128)}) %all-gather.4.cloned.1.call-update) | async-done | bytes 1638416 | tf_op jit(solution)/shard_map/all_gather | solution.py:71
  79.0 2.5 fusion.10
  81.6 0.8 fusion.19
  82.4 1.1 fusion.27
  83.4 2.1 multiply_reduce_fusion
  85.5 0.0 all-reduce.5.cloned.1.call-update
  85.6 0.2 all-reduce.7.cloned.1.call-start
  85.8 3.5 subtract_multiply_fusion
  89.3 7.4 %scatter_custom_fusion = f32[512,1024]{1,0:T(8,128)} fusion(s32[512]{0:T(512)S(1)} %bitcast.51, f32[512,1024]{1,0:T(8,128)} %subtract_multiply_fusion, f32[]{:T(128)} %constant.19.clone.1, f32[512]{0:T(512)S(1)} %bitcast.42), kind=kCustom, calls=%fused_computation.14 | custom fusion | flops 1048576 | bytes 4196356 | tf_op jit(solution)/shard_map/scatter-add | solution.py:94
  96.7 7.8 %scatter_custom_fusion.1 = f32[512,1024]{1,0:T(8,128)} fusion(f32[512,1024]{1,0:T(8,128)} %scatter_custom_fusion, s32[512]{0:T(512)S(1)} %bitcast.50, f32[512,1024]{1,0:T(8,128)S(1)} %copy-done.1, f32[512]{0:T(512)S(1)} %bitcast.40), kind=kCustom, calls=%fused_computation.12 | custom fusion | flops 1048576 | bytes 4196352 | tf_op jit(solution)/shard_map/scatter-add | solution.py:94
  104.5 7.8 %scatter_custom_fusion.2 = f32[512,1024]{1,0:T(8,128)} fusion(f32[512,1024]{1,0:T(8,128)} %scatter_custom_fusion.1, s32[512]{0:T(512)S(1)} %bitcast.49, f32[512,1024]{1,0:T(8,128)S(1)} %copy-done.1, f32[512]{0:T(512)S(1)} %bitcast.38), kind=kCustom, calls=%fused_computation.10 | custom fusion | flops 1048576 | bytes 4196352 | tf_op jit(solution)/shard_map/scatter-add | solution.py:94
  112.3 1.9 convert.6
  114.2 1.3 collective-permute-start.2
  115.5 1.3 collective-permute-start.3
  116.8 46.8 %all-reduce.5.cloned.1.call-done = f32[100,1024]{1,0:T(8,128)} async-done(((f32[100,1024]{1,0:T(8,128)}), f32[100,1024]{1,0:T(8,128)}) %all-reduce.5.cloned.1.call-update) | async-done | bytes 409616 | tf_op jit(solution)/shard_map/psum | solution.py:100
  163.6 0.0 all-reduce.7.cloned.1.call-update
  165.0 19.6 %all-reduce.1 = (f32[]{:T(128)}, f32[1024]{0:T(1024)S(1)}) all-reduce(f32[]{:T(128)S(6)} %sub.46, f32[1024]{0:T(1024)S(1)} %get-tuple-element.5), channel_id=1, replica_groups=mesh['member'=8,'grid'=32] {'member'}, use_global_device_ids=true, to_apply=%region_6.8 | all-reduce | flops 1025 | bytes 8200 | tf_op jit(solution)/shard_map/psum | solution.py:100
  184.5 66.7 %all-reduce = (f32[]{:T(128)}, f32[1024]{0:T(1024)}) all-reduce(f32[]{:T(128)} %get-tuple-element.14, f32[1024]{0:T(1024)S(1)} %get-tuple-element.15), channel_id=1, replica_groups=mesh['member'=8,'grid'=32] {'grid'}, use_global_device_ids=true, to_apply=%region_7.9 | all-reduce | flops 1025 | bytes 8200 | tf_op jit(solution)/shard_map/psum | solution.py:100
  251.9 0.0 collective-permute-done.2
  251.9 0.0 collective-permute-done.3
  251.9 0.9 fusion.17
  252.9 173.8 %all-reduce.7.cloned.1.call-done = f32[100,1024]{1,0:T(8,128)} async-done(((f32[100,1024]{1,0:T(8,128)}), f32[100,1024]{1,0:T(8,128)}) %all-reduce.7.cloned.1.call-update) | async-done | bytes 409616 | tf_op jit(solution)/shard_map/psum | solution.py:100
  426.7 1.8 copy.20
  (29 shorter events, 0.1 us)
Async XLA Ops:
  7.2 20.7 %copy-start = (bf16[100,1024]{1,0:T(8,128)(2,1)S(1)}, bf16[100,1024]{1,0:T(8,128)(2,1)}, u32[]{:S(2)}) copy-start(bf16[100,1024]{1,0:T(8,128)(2,1)} %param.20) | copy-start | bytes 614404
  7.2 71.9 %all-gather.4.cloned.1.call-start = ((), (), s32[]{:S(2)}) async-start(), calls=%async_computation.2 | async-start | bytes 1916928 | tf_op jit(solution)/shard_map/all_gather | solution.py:71
  8.3 5.4 %collective-permute-start = (bf16[1,128,1024]{2,1,0:T(8,128)(2,1)S(1)}, bf16[1,128,1024]{2,1,0:T(8,128)(2,1)S(1)}, u32[]{:S(2)}, u32[]{:S(2)}) collective-permute-start(bf16[1,128,1024]{2,1,0:T(8,128)(2,1)S(1)} %get-tuple-element.20), channel_id=1, source_target_pairs={{0,1},{1,2},{2,3},{3,4},{4,5},{5,6},{6,7},{7,8},{8,9},{9,10},{10,1... | collective-permute-start | bytes 786440 | tf_op jit(solution)/shard_map/ppermute | solution.py:18
  10.1 5.1 %collective-permute-start.1 = (bf16[1,128,1024]{2,1,0:T(8,128)(2,1)S(1)}, bf16[1,128,1024]{2,1,0:T(8,128)(2,1)S(1)}, u32[]{:S(2)}, u32[]{:S(2)}) collective-permute-start(bf16[1,128,1024]{2,1,0:T(8,128)(2,1)S(1)} %get-tuple-element.21), channel_id=1, source_target_pairs={{1,0},{2,1},{3,2},{4,3},{5,4},{6,5},{7,6},{8,7},{9,8},{10,9},{11,1... | collective-permute-start | bytes 786440 | tf_op jit(solution)/shard_map/ppermute | solution.py:19
  26.8 0.7 copy-start.6
  27.2 0.9 copy-start.4
  27.5 1.8 copy-start.7
  28.1 53.4 %copy-start.8 = (f32[512]{0:T(512)S(1)}, f32[512]{0:T(512)}, u32[]{:S(2)}) copy-start(f32[512]{0:T(512)} %param.18) | copy-start | bytes 6148
  28.1 53.4 %copy-start.9 = (f32[100]{0:T(128)S(1)}, f32[100]{0:T(128)}, u32[]{:S(2)}) copy-start(f32[100]{0:T(128)} %param.19) | copy-start | bytes 1204
  29.3 134.3 %all-reduce.5.cloned.1.call-start = ((), (), s32[]{:S(2)}) async-start(), calls=%async_computation | async-start | bytes 851968 | tf_op jit(solution)/shard_map/psum | solution.py:100
  79.0 2.5 copy-start.3
  79.0 2.5 copy-start.5
  85.6 341.1 %all-reduce.7.cloned.1.call-start = ((), (), s32[]{:S(2)}) async-start(), calls=%async_computation.1 | async-start | bytes 851968 | tf_op jit(solution)/shard_map/psum | solution.py:100
  89.3 7.5 %copy-start.1 = (f32[512,1024]{1,0:T(8,128)S(1)}, f32[512,1024]{1,0:T(8,128)}, u32[]{:S(2)}) copy-start(f32[512,1024]{1,0:T(8,128)} %subtract_multiply_fusion) | copy-start | bytes 6291460
  112.3 139.6 %copy-start.2 = (f32[512,1024]{1,0:T(8,128)S(1)}, f32[512,1024]{1,0:T(8,128)}, u32[]{:S(2)}) copy-start(f32[512,1024]{1,0:T(8,128)} %scatter_custom_fusion.2) | copy-start | bytes 6291460
  114.2 137.7 %collective-permute-start.2 = (bf16[128,1024]{1,0:T(8,128)(2,1)S(1)}, bf16[128,1024]{1,0:T(8,128)(2,1)S(1)}, u32[]{:S(2)}, u32[]{:S(2)}) collective-permute-start(bf16[128,1024]{1,0:T(8,128)(2,1)S(1)} %get-tuple-element.18), channel_id=1, source_target_pairs={{0,1},{1,2},{2,3},{3,4},{4,5},{5,6},{6,7},{7,8},{8,9},{9,10},{10,1... | collective-permute-start | bytes 786440 | tf_op jit(solution)/shard_map/ppermute | solution.py:27
  115.5 136.4 %collective-permute-start.3 = (bf16[128,1024]{1,0:T(8,128)(2,1)S(1)}, bf16[128,1024]{1,0:T(8,128)(2,1)S(1)}, u32[]{:S(2)}, u32[]{:S(2)}) collective-permute-start(bf16[128,1024]{1,0:T(8,128)(2,1)S(1)} %get-tuple-element.19), channel_id=1, source_target_pairs={{1,0},{2,1},{3,2},{4,3},{5,4},{6,5},{7,6},{8,7},{9,8},{10,9},{11,1... | collective-permute-start | bytes 786440 | tf_op jit(solution)/shard_map/ppermute | solution.py:27
Sparse Core Ops, SparseCore 0:
  29.4 49.5 all-gather.3
  85.7 77.8 all-reduce.4
  166.5 260.1 all-reduce.6
